TPU v7x, 256 devices: a whole 4x4x8 slice. The times are simulated.
256 devices in a mesh: seq: 128 (over z, x, y), chan: 2 (over core).
Axes of the slice: x: 4, y: 4, z: 8, core: 2. Of those that a mesh axis runs over, the one named last changes fastest.
Arguments:
- signal: bfloat16 [32768, 512], P('seq', 'chan'), may hold values from -6 to 6
- gating: bfloat16 [32768, 512], P('seq', 'chan'), may hold values from -6 to 6
- cotangent: bfloat16 [32768, 512], P('seq', 'chan'), may hold values from -6 to 6
- decay_rates: float32 [512], P('chan'), may hold values from 3.0517577e-07 to 0.03
- skip_gain: float32 [512], P('chan'), may hold values from 0.5 to 1.5
- first_weight: float32 [33, 64], replicated, may hold values from -1 to 1
- first_bias: float32 [64], replicated, may hold values from -3.140625 to 3.140625
- second_weight: float32 [64, 64], replicated, may hold values from -0.75 to 0.75
- second_bias: float32 [64], replicated, may hold values from -3.140625 to 3.140625
- third_weight: float32 [64, 512], P(None, 'chan'), may hold values from -0.75 to 0.75
Outputs:
- output: bfloat16 [32768, 512], P('seq', 'chan')
- grad_signal: bfloat16 [32768, 512], P('seq', 'chan')
- grad_gating: bfloat16 [32768, 512], P('seq', 'chan')
- grad_skip: float32 [512], P('chan')
- grad_first_weight: float32 [33, 64], replicated
- grad_first_bias: float32 [64], replicated
- grad_second_weight: float32 [64, 64], replicated
- grad_second_bias: float32 [64], replicated
- grad_third_weight: float32 [64, 512], P(None, 'chan')
All inputs are finite; a program needn't handle non-finite values.
Results may differ from a plain program's by a relative error of at most 0.001.
Values may be sent and summed in bfloat16 or wider, within the bound.
A program may use at most 128 MiB of HBM per device.

v0:
```python
import math

import jax
import jax.experimental.pallas as pl
import jax.experimental.pallas.tpu as pltpu
import jax.numpy as jnp
import ml_dtypes
import numpy as np
from jax import lax
from jax.sharding import PartitionSpec as P

BANDS = 16
ROWS = 256
PARTS = 128
HALF = 128
LENGTH = ROWS * PARTS
FULL = 2 * LENGTH
FH = 64
EMB = 33

full_turn = 2.0 * math.pi
norm_eps = 1e-06
MESH = pl.DeviceIdType.MESH
BF = jnp.bfloat16
F32 = jnp.float32


def pieces(table):
    high = table.astype(ml_dtypes.bfloat16)
    low = (table - high.astype(np.float64)).astype(ml_dtypes.bfloat16)
    return high, low


def tables():
    freq = np.arange(HALF) + 0.5
    block = np.arange(PARTS)
    inner = np.arange(ROWS)
    outer_angle = full_turn * ((freq[:, None] * block[None, :]) % 256) / 256
    outer = np.concatenate([np.cos(outer_angle), -np.sin(outer_angle)], axis=0)
    back = outer.T * (2.0 / FULL)
    inner_angle = full_turn * ((inner[:, None] * inner[None, :]) % ROWS) / ROWS
    both = np.concatenate([np.cos(inner_angle), np.sin(inner_angle)], axis=1)
    twist = full_turn * (freq[:, None] * inner[None, :]) / FULL
    return (
        *pieces(outer),
        *pieces(back),
        *pieces(both),
        np.cos(twist).astype(np.float32),
        np.sin(twist).astype(np.float32),
    )


def split(arr):
    high = arr.astype(BF)
    return high, (arr - high.astype(F32)).astype(BF)


def dot(left, right):
    return jnp.dot(left, right, preferred_element_type=F32)


def dot3(left, right):
    return dot(left[0], right[0]) + dot(left[0], right[1]) + dot(left[1], right[0])


def contract(left, right, dims, precision):
    return lax.dot_general(
        left, right, ((dims[:1], dims[1:]), ((), ())), precision=precision, preferred_element_type=F32
    )


def total(arr):
    return jnp.sum(arr, axis=(0, 1), keepdims=True)


def kernel(
    signal,
    gating,
    cotangent,
    decay,
    skip_row,
    skip_all,
    w1,
    b1,
    w2,
    b2,
    w3,
    outer_hi,
    outer_lo,
    back_hi,
    back_lo,
    both_hi,
    both_lo,
    twist_cos,
    twist_sin,
    output,
    grad_signal,
    grad_gating,
    grad_skip,
    grad_w1,
    grad_b1,
    grad_w2,
    grad_b2,
    grad_w3,
    w1s,
    w2s,
    emb,
    firstx,
    second,
    cos1,
    cos2,
    fade,
    wide,
    stage,
    send_a,
    recv_a,
    send_b,
    recv_b,
    send_c,
    recv_c,
    send_d,
    recv_d,
    send_e,
    recv_e,
    mine,
    other,
    send_f,
    recv_f,
    spec,
    vals,
    dfilt,
    send_sems,
    recv_sems,
):
    me = lax.axis_index("seq")
    core = lax.axis_index("chan")
    barrier = pltpu.get_barrier_semaphore()

    @pl.loop(1, PARTS)
    def _(step):
        pl.semaphore_signal(
            barrier, inc=1, device_id={"seq": lax.rem(me + step, PARTS)}, device_id_type=MESH
        )

    pl.semaphore_signal(barrier, inc=1, device_id={"chan": 1 - core}, device_id_type=MESH)

    def spread(src_of, own, recv, at):
        @pl.loop(1, PARTS)
        def _(step):
            dst = lax.rem(me + step, PARTS)
            pltpu.make_async_remote_copy(
                src_ref=src_of(dst),
                dst_ref=recv.at[me],
                send_sem=send_sems.at[at],
                recv_sem=recv_sems.at[at],
                device_id={"seq": dst},
                device_id_type=MESH,
            ).start()

        pltpu.make_async_copy(own, recv.at[me], recv_sems.at[at]).start()

    def arrived(recv, at):
        pltpu.make_async_copy(recv, recv, recv_sems.at[at]).wait()

    def left(recv, at):
        rest = recv.at[pl.ds(0, PARTS - 1)]
        pltpu.make_async_copy(rest, rest, send_sems.at[at]).wait()

    def place(plane, arr):
        for q in range(2):
            for h in range(2):
                stage[:, 2 * q + h, plane * 128 : plane * 128 + 128] = arr[
                    q * 128 : q * 128 + 128, h * 128 : h * 128 + 128
                ]

    def put(plane, q, arr):
        for h in range(2):
            stage[:, 2 * q + h, plane * 128 : plane * 128 + 128] = arr[:, h * 128 : h * 128 + 128]

    def take(plane, q):
        return jnp.concatenate(
            [stage[:, 2 * q + h, plane * 128 : plane * 128 + 128] for h in range(2)], axis=1
        )

    place(0, signal[...].astype(F32).T)
    dmixed_rows = cotangent[...].astype(F32) * gating[...].astype(F32)
    wide[...] = dmixed_rows.T
    high = wide[...].astype(BF).astype(F32)
    place(1, high)
    place(2, wide[...] - high)
    send_a[...] = stage[...].astype(BF)

    stamp = me * ROWS + lax.broadcasted_iota(jnp.int32, (BANDS, ROWS), 1)
    band = lax.broadcasted_iota(jnp.int32, (BANDS, ROWS), 0) + 1
    phase = ((stamp * band) & (LENGTH - 1)).astype(F32) * (full_turn / LENGTH)
    emb[0:16, :] = jnp.cos(phase)
    emb[16:32, :] = jnp.sin(phase)
    line = lax.broadcasted_iota(jnp.int32, (8, ROWS), 0)
    ramp = stamp[0:8].astype(F32)
    emb[32:40, :] = jnp.where(line == 0, ramp / LENGTH, jnp.where(line == 1, 1.0, 0.0))
    w1s[0:32, :] = w1[1:33, :]
    w1s[32:40, :] = jnp.zeros((8, FH), F32)
    w1s[32:33, :] = w1[0:1, :]
    w1s[33:34, :] = b1[...]
    w2s[0:64, :] = w2[...]
    w2s[64:72, :] = jnp.zeros((8, FH), F32)
    w2s[64:65, :] = b2[...]
    pre1 = contract(w1s[...], emb[...], (0, 0), lax.Precision.HIGHEST)
    firstx[0:64, :] = jnp.sin(pre1)
    firstx[64:72, :] = jnp.where(line == 0, 1.0, 0.0)
    cos1[...] = jnp.cos(pre1)
    pre2 = contract(w2s[...], firstx[...], (0, 0), lax.Precision.HIGHEST)
    second[...] = jnp.sin(pre2)
    cos2[...] = jnp.cos(pre2)
    rates = jnp.broadcast_to(decay[...], (ROWS, ROWS)).T
    fade[...] = jnp.exp(-jnp.broadcast_to(ramp[0:1], (ROWS, ROWS)) * rates)
    wide[...] = contract(w3[...], second[...], (0, 0), lax.Precision.HIGHEST) * fade[...]
    high = wide[...].astype(BF).astype(F32)
    place(0, high)
    place(1, wide[...] - high)
    send_b[...] = stage[:, :, 0:256].astype(BF)

    pl.semaphore_wait(barrier, PARTS)
    spread(lambda dst: send_a.at[dst], send_a.at[me], recv_a, 0)
    spread(lambda dst: send_b.at[dst], send_b.at[me], recv_b, 1)

    both = (both_hi, both_lo)

    def forward(slot, parts):
        if len(parts) == 1:
            rows = dot(outer_hi[...], parts[0]) + dot(outer_lo[...], parts[0])
        else:
            rows = dot3((outer_hi[...], outer_lo[...]), parts)
        real, imag = rows[0:HALF], rows[HALF:]
        turned = jnp.concatenate(
            [
                real * twist_cos[...] + imag * twist_sin[...],
                imag * twist_cos[...] - real * twist_sin[...],
            ],
            axis=0,
        )
        out = dot3(split(turned), (both_hi[...], both_lo[...]))
        spec[slot, 0] = out[0:HALF, 0:ROWS] + out[HALF:, ROWS:]
        spec[slot, 1] = out[HALF:, 0:ROWS] - out[0:HALF, ROWS:]

    def inverse(real, imag):
        out = dot3(split(jnp.concatenate([real, imag], axis=0)), (both_hi[...], both_lo[...]))
        mid_real = out[0:HALF, 0:ROWS] - out[HALF:, ROWS:]
        mid_imag = out[HALF:, 0:ROWS] + out[0:HALF, ROWS:]
        turned = jnp.concatenate(
            [
                mid_real * twist_cos[...] - mid_imag * twist_sin[...],
                mid_imag * twist_cos[...] + mid_real * twist_sin[...],
            ],
            axis=0,
        )
        return dot3((back_hi[...], back_lo[...]), split(turned))

    arrived(recv_a, 0)
    stage[...] = recv_a[...].astype(F32)
    skip_grads = []
    for q in range(2):
        sig = take(0, q)
        high, low = take(1, q), take(2, q)
        vals[q] = high + low
        skip_grads.append(total(vals[q] * sig))
        forward(q, (sig.astype(BF),))
        forward(2 + q, (high.astype(BF), low.astype(BF)))
    for q in range(2):
        sig_re, sig_im, dm_re, dm_im = spec[q, 0], spec[q, 1], spec[2 + q, 0], spec[2 + q, 1]
        dfilt[q] = inverse(sig_re * dm_re + sig_im * dm_im, sig_re * dm_im - sig_im * dm_re)

    arrived(recv_b, 1)
    stage[:, :, 0:256] = recv_b[...].astype(F32)
    filters, scales = [], []
    for q in range(2):
        high, low = take(0, q), take(1, q)
        shaped = high + low
        scale = 1.0 / jnp.sqrt(total(shaped * shaped) + norm_eps)
        filt = shaped * scale
        filters.append((high.astype(BF), low.astype(BF)))
        scales.append(scale)
        dfilt[q] = (dfilt[q] - filt * total(filt * dfilt[q])) * scale
    for q in range(2):
        high = dfilt[q].astype(BF).astype(F32)
        put(0, q, high)
        put(1, q, dfilt[q] - high)
    send_c[...] = stage[:, :, 0:256].astype(BF)
    spread(lambda dst: send_c.at[dst], send_c.at[me], recv_c, 2)

    for q in range(2):
        forward(4 + q, filters[q])
    for q in range(2):
        filt_re, filt_im = spec[4 + q, 0] * scales[q], spec[4 + q, 1] * scales[q]
        sig_re, sig_im, dm_re, dm_im = spec[q, 0], spec[q, 1], spec[2 + q, 0], spec[2 + q, 1]
        conv = inverse(sig_re * filt_re - sig_im * filt_im, sig_re * filt_im + sig_im * filt_re)
        high = conv.astype(BF).astype(F32)
        put(0, q, high)
        put(1, q, conv - high)
        corr = inverse(filt_re * dm_re + filt_im * dm_im, filt_re * dm_im - filt_im * dm_re)
        put(2, q, corr + skip_all[me + q * PARTS] * vals[q])
    send_d[...] = stage[...].astype(BF)
    spread(lambda dst: send_d.at[dst], send_d.at[me], recv_d, 3)

    arrived(recv_c, 2)
    stage[:, :, 0:256] = recv_c[...].astype(F32)
    for q in range(2):
        wide[q * 128 : q * 128 + 128, :] = take(0, q) + take(1, q)
    wide[...] = wide[...] * fade[...]
    draw = wide[...]
    third = contract(draw, second[...], (1, 1), lax.Precision.HIGH)
    dpre2 = contract(w3[...], draw, (1, 0), lax.Precision.HIGH) * cos2[...]
    grad2 = contract(firstx[...], dpre2, (1, 1), lax.Precision.HIGH)
    dpre1 = contract(w2[...], dpre2, (1, 0), lax.Precision.HIGH) * cos1[...]
    grad1 = contract(emb[...], dpre1, (1, 1), lax.Precision.HIGH)
    send_e[:, 0, :] = jnp.concatenate([third[0:128], third[128:256]], axis=1)
    shared = jnp.concatenate([grad1, grad2, jnp.zeros((16, FH), F32)], axis=0)
    send_e[:, 1, :] = jnp.concatenate([shared, jnp.zeros((128, FH), F32)], axis=1)
    spread(lambda dst: send_e.at[dst], send_e.at[me], recv_e, 4)
    arrived(recv_e, 4)
    summed = jnp.sum(recv_e[...], axis=0)
    mine[...] = summed
    swap = pltpu.make_async_remote_copy(
        src_ref=mine,
        dst_ref=other,
        send_sem=send_sems.at[5],
        recv_sem=recv_sems.at[5],
        device_id={"chan": 1 - core},
        device_id_type=MESH,
    )
    swap.start()
    swap.wait()
    lane = lax.broadcasted_iota(jnp.int32, (1, 128), 1)
    send_f[0:1, :] = summed[0:1]
    send_f[1:2, :] = jnp.where(
        lane < FH,
        summed[1:2] + other[1:2, :],
        jnp.where(lane == FH, skip_grads[0], skip_grads[1]),
    )
    spread(lambda dst: send_f, send_f, recv_f, 6)

    arrived(recv_d, 3)
    stage[...] = recv_d[...].astype(F32)
    for q in range(2):
        wide[q * 128 : q * 128 + 128, :] = take(0, q) + take(1, q)
    mixed = wide[...].T + skip_row[...] * signal[...].astype(F32)
    output[...] = (gating[...].astype(F32) * mixed).astype(BF)
    grad_gating[...] = (cotangent[...].astype(F32) * mixed).astype(BF)
    for q in range(2):
        wide[q * 128 : q * 128 + 128, :] = take(2, q)
    grad_signal[...] = wide[...].T.astype(BF)

    arrived(recv_f, 6)
    thirds = recv_f[:, 0, :].T
    grad_w3[:, 0:128] = thirds[0:64]
    grad_w3[:, 128:256] = thirds[64:128]
    rest = recv_f[:, 1, :]
    skips = rest.T
    grad_skip[:, 0:128] = skips[64:65]
    grad_skip[:, 128:256] = skips[65:66]
    grad_w1[1:33, :] = rest[0:32, 0:64]
    grad_w1[0:1, :] = rest[32:33, 0:64]
    grad_b1[...] = rest[33:34, 0:64]
    grad_w2[...] = rest[40:104, 0:64]
    grad_b2[...] = rest[104:105, 0:64]

    left(send_a, 0)
    left(send_b, 1)
    left(send_c, 2)
    left(send_d, 3)
    left(send_e, 4)
    left(recv_f, 6)


def body(
    signal,
    gating,
    cotangent,
    decay_rates,
    skip_gain,
    first_weight,
    first_bias,
    second_weight,
    second_bias,
    third_weight,
):
    vmem = pl.BlockSpec(memory_space=pltpu.VMEM)
    smem = pl.BlockSpec(memory_space=pltpu.SMEM)
    consts = [jnp.asarray(t) for t in tables()]
    wide_msg = pltpu.VMEM((PARTS, 4, 384), BF)
    thin_msg = pltpu.VMEM((PARTS, 4, 256), BF)
    pair = pltpu.VMEM((2, 128), F32)
    results = pl.pallas_call(
        kernel,
        out_shape=[
            jax.ShapeDtypeStruct((ROWS, ROWS), BF),
            jax.ShapeDtypeStruct((ROWS, ROWS), BF),
            jax.ShapeDtypeStruct((ROWS, ROWS), BF),
            jax.ShapeDtypeStruct((1, ROWS), F32),
            jax.ShapeDtypeStruct((EMB, FH), F32),
            jax.ShapeDtypeStruct((1, FH), F32),
            jax.ShapeDtypeStruct((FH, FH), F32),
            jax.ShapeDtypeStruct((1, FH), F32),
            jax.ShapeDtypeStruct((FH, ROWS), F32),
        ],
        in_specs=[vmem] * 5 + [smem] + [vmem] * 13,
        out_specs=[vmem] * 9,
        scratch_shapes=[
            pltpu.VMEM((40, FH), F32),
            pltpu.VMEM((72, FH), F32),
            pltpu.VMEM((40, ROWS), F32),
            pltpu.VMEM((72, ROWS), F32),
            pltpu.VMEM((FH, ROWS), F32),
            pltpu.VMEM((FH, ROWS), F32),
            pltpu.VMEM((FH, ROWS), F32),
            pltpu.VMEM((ROWS, ROWS), F32),
            pltpu.VMEM((ROWS, ROWS), F32),
            pltpu.VMEM((PARTS, 4, 384), F32),
            wide_msg,
            wide_msg,
            thin_msg,
            thin_msg,
            thin_msg,
            thin_msg,
            wide_msg,
            wide_msg,
            pltpu.VMEM((PARTS, 2, 128), F32),
            pltpu.VMEM((PARTS, 2, 128), F32),
            pair,
            pair,
            pair,
            pltpu.VMEM((PARTS, 2, 128), F32),
            pltpu.VMEM((6, 2, HALF, ROWS), F32),
            pltpu.VMEM((2, PARTS, ROWS), F32),
            pltpu.VMEM((2, PARTS, ROWS), F32),
            pltpu.SemaphoreType.DMA((7,)),
            pltpu.SemaphoreType.DMA((7,)),
        ],
        compiler_params=pltpu.CompilerParams(
            collective_id=0, has_side_effects=True, vmem_limit_bytes=48 << 20
        ),
        name="hyena",
    )(
        signal,
        gating,
        cotangent,
        decay_rates.reshape(1, ROWS),
        skip_gain.reshape(1, ROWS),
        skip_gain,
        first_weight,
        first_bias.reshape(1, FH),
        second_weight,
        second_bias.reshape(1, FH),
        third_weight,
        *consts,
    )
    out, g_sig, g_gate, g_skip, g_w1, g_b1, g_w2, g_b2, g_w3 = results
    return (
        out,
        g_sig,
        g_gate,
        g_skip.reshape(ROWS),
        g_w1,
        g_b1.reshape(FH),
        g_w2,
        g_b2.reshape(FH),
        g_w3,
    )


def solution(mesh):
    return jax.shard_map(
        body,
        mesh=mesh,
        in_specs=(
            P("seq", "chan"),
            P("seq", "chan"),
            P("seq", "chan"),
            P("chan"),
            P("chan"),
            P(),
            P(),
            P(),
            P(),
            P(None, "chan"),
        ),
        out_specs=(
            P("seq", "chan"),
            P("seq", "chan"),
            P("seq", "chan"),
            P("chan"),
            P(),
            P(),
            P(),
            P(),
            P(None, "chan"),
        ),
        check_vma=False,
    )
```

profile of v0, /device:TPU:1, one launch (start us, length us, event | category | flops | bytes accessed | tf_op | source)
XLA Modules:
  0.0 85.1 jit_solution(7916220696600431562)
XLA Ops:
  0.6 0.0 copy-start.15
  0.7 0.0 copy-start.17
  0.7 0.0 copy-start.14
  0.7 0.0 copy-start.16
  0.7 0.6 copy-done.15
  1.3 0.0 copy-done.17
  1.3 0.0 copy-done.14
  1.4 0.0 copy-done.16
  1.4 0.0 copy-start
  1.4 0.9 %copy-done = bf16[256,512]{1,0:T(8,128)(2,1)S(1)} copy-done((bf16[256,512]{1,0:T(8,128)(2,1)S(1)}, bf16[256,512]{1,0:T(8,128)(2,1)}, u32[]{:S(2)}) %copy-start) | copy-done | bytes 262168
  2.3 0.0 copy-start.1
  2.3 0.9 %copy-done.1 = bf16[256,512]{1,0:T(8,128)(2,1)S(1)} copy-done((bf16[256,512]{1,0:T(8,128)(2,1)S(1)}, bf16[256,512]{1,0:T(8,128)(2,1)}, u32[]{:S(2)}) %copy-start.1) | copy-done | bytes 262168
  3.3 0.0 copy-start.2
  3.3 0.9 %copy-done.2 = bf16[256,256]{1,0:T(8,128)(2,1)S(1)} copy-done((bf16[256,256]{1,0:T(8,128)(2,1)S(1)}, bf16[256,256]{1,0:T(8,128)(2,1)}, u32[]{:S(2)}) %copy-start.2) | copy-done | bytes 131096
  4.2 0.0 copy-start.3
  4.2 0.9 %copy-done.3 = bf16[256,256]{1,0:T(8,128)(2,1)S(1)} copy-done((bf16[256,256]{1,0:T(8,128)(2,1)S(1)}, bf16[256,256]{1,0:T(8,128)(2,1)}, u32[]{:S(2)}) %copy-start.3) | copy-done | bytes 131096
  5.1 0.0 copy-start.4
  5.1 0.9 %copy-done.4 = bf16[256,256]{1,0:T(8,128)(2,1)S(1)} copy-done((bf16[256,256]{1,0:T(8,128)(2,1)S(1)}, bf16[256,256]{1,0:T(8,128)(2,1)}, u32[]{:S(2)}) %copy-start.4) | copy-done | bytes 131096
  6.0 0.0 copy-start.5
  6.0 0.9 %copy-done.5 = f32[128,256]{1,0:T(8,128)S(1)} copy-done((f32[128,256]{1,0:T(8,128)S(1)}, f32[128,256]{1,0:T(8,128)}, u32[]{:S(2)}) %copy-start.5) | copy-done | bytes 131096
  6.9 0.0 copy-start.6
  6.9 0.9 %copy-done.6 = f32[128,256]{1,0:T(8,128)S(1)} copy-done((f32[128,256]{1,0:T(8,128)S(1)}, f32[128,256]{1,0:T(8,128)}, u32[]{:S(2)}) %copy-start.6) | copy-done | bytes 131096
  7.8 0.0 copy-start.7
  7.8 0.8 copy-done.7
  8.6 0.0 copy-start.8
  8.6 0.8 copy-done.8
  9.5 0.0 copy-start.9
  9.5 0.8 copy-done.9
  10.3 0.0 copy-start.10
  10.3 0.8 copy-done.10
  11.1 0.0 copy-start.11
  11.1 0.8 copy-done.11
  12.0 0.0 copy-start.12
  12.0 0.8 copy-done.12
  12.7 0.0 copy-start.13
  12.7 0.7 copy-done.13
  13.5 66.2 %hyena.1 = (bf16[256,256]{1,0:T(8,128)(2,1)S(1)}, bf16[256,256]{1,0:T(8,128)(2,1)S(1)}, bf16[256,256]{1,0:T(8,128)(2,1)S(1)}, f32[1,256]{1,0:T(1,128)S(1)}, f32[...) custom-call(bf16[256,256]{1,0:T(8,128)(2,1)S(1)} %copy-done.2, ...), custom_call_target="tpu_custom_call" | custom-call | tf_op jit(solution)/shard_map/hyena/pallas_call | solution.py:393
  79.7 0.7 copy.36
  80.3 0.7 copy.37
  81.0 0.7 copy.38
  81.6 0.6 copy.39
  82.2 0.6 copy.40
  82.8 0.5 copy.41
  83.3 0.6 copy.42
  83.9 0.5 copy.43
  84.5 0.6 copy.44
Async XLA Ops:
  0.6 0.7 copy-start.15
  0.7 0.7 copy-start.17
  0.7 0.7 copy-start.14
  0.7 0.7 copy-start.16
  1.4 1.0 %copy-start = (bf16[256,512]{1,0:T(8,128)(2,1)S(1)}, bf16[256,512]{1,0:T(8,128)(2,1)}, u32[]{:S(2)}) copy-start(bf16[256,512]{1,0:T(8,128)(2,1)} %constant.21.clone.both_lo) | copy-start | bytes 786436
  2.3 0.9 %copy-start.1 = (bf16[256,512]{1,0:T(8,128)(2,1)S(1)}, bf16[256,512]{1,0:T(8,128)(2,1)}, u32[]{:S(2)}) copy-start(bf16[256,512]{1,0:T(8,128)(2,1)} %constant.20.clone.both_hi) | copy-start | bytes 786436
  3.3 0.9 %copy-start.2 = (bf16[256,256]{1,0:T(8,128)(2,1)S(1)}, bf16[256,256]{1,0:T(8,128)(2,1)}, u32[]{:S(2)}) copy-start(bf16[256,256]{1,0:T(8,128)(2,1)} %signal.1) | copy-start | bytes 393220
  4.2 0.9 %copy-start.3 = (bf16[256,256]{1,0:T(8,128)(2,1)S(1)}, bf16[256,256]{1,0:T(8,128)(2,1)}, u32[]{:S(2)}) copy-start(bf16[256,256]{1,0:T(8,128)(2,1)} %gating.1) | copy-start | bytes 393220
  5.1 0.9 %copy-start.4 = (bf16[256,256]{1,0:T(8,128)(2,1)S(1)}, bf16[256,256]{1,0:T(8,128)(2,1)}, u32[]{:S(2)}) copy-start(bf16[256,256]{1,0:T(8,128)(2,1)} %cotangent.1) | copy-start | bytes 393220
  6.0 0.9 %copy-start.5 = (f32[128,256]{1,0:T(8,128)S(1)}, f32[128,256]{1,0:T(8,128)}, u32[]{:S(2)}) copy-start(f32[128,256]{1,0:T(8,128)} %constant.23.clone.twist_sin) | copy-start | bytes 393220
  6.9 0.9 %copy-start.6 = (f32[128,256]{1,0:T(8,128)S(1)}, f32[128,256]{1,0:T(8,128)}, u32[]{:S(2)}) copy-start(f32[128,256]{1,0:T(8,128)} %constant.22.clone.twist_cos) | copy-start | bytes 393220
  7.8 0.8 copy-start.7
  8.6 0.8 copy-start.8
  9.5 0.8 copy-start.9
  10.3 0.8 copy-start.10
  11.1 0.8 copy-start.11
  12.0 0.8 copy-start.12
  12.7 0.7 copy-start.13
where the time goes:
time: 85.7 us; the launch traced here: 85.1 us
  Pallas kernels  66.2 us (77%)
  local copies, waits for them, and re-layouts  18.2 us (21%)
    pallas_call x1, Pallas kernels, body(): pl.pallas_call(kernel, out_shape=[jax.ShapeDtypeStruct((ROWS, ROWS), BF),...  66.2 us
    unnamed x45, local copies, waits for them, and re-layouts  18.2 us

commit v1 on v0

--- a/solution.py
+++ b/solution.py
@@ -15,6 +15,7 @@
 HALF = 128
 LENGTH = ROWS * PARTS
 FULL = 2 * LENGTH
+LIMIT = 64 << 20
 FH = 64
 EMB = 33
 
@@ -73,13 +74,54 @@
     return jnp.sum(arr, axis=(0, 1), keepdims=True)
 
 
+def deliver(*refs):
+    count = len(refs) // 3
+    heard, told = refs[-2:]
+    ins, outs, held = refs[:count], refs[count : 2 * count], refs[2 * count : 3 * count]
+    loads = [pltpu.make_async_copy(ins[at], held[at], heard.at[at]) for at in range(count)]
+    stores = [pltpu.make_async_copy(held[at], outs[at], told.at[at]) for at in range(count)]
+    for load in loads:
+        load.start()
+    for load, store in zip(loads, stores):
+        load.wait()
+        store.start()
+    for store in stores:
+        store.wait()
+
+
 def kernel(
+    signal_far,
+    gating_far,
+    cotangent_far,
+    decay_far,
+    skip_row_far,
+    w1_far,
+    b1_far,
+    w2_far,
+    b2_far,
+    w3_far,
+    outer_hi_far,
+    outer_lo_far,
+    back_hi_far,
+    back_lo_far,
+    both_hi_far,
+    both_lo_far,
+    twist_cos_far,
+    twist_sin_far,
+    output,
+    grad_signal,
+    grad_gating,
+    grad_skip,
+    grad_w1,
+    grad_b1,
+    grad_w2,
+    grad_b2,
+    grad_w3,
     signal,
     gating,
     cotangent,
     decay,
     skip_row,
-    skip_all,
     w1,
     b1,
     w2,
@@ -93,15 +135,7 @@
     both_lo,
     twist_cos,
     twist_sin,
-    output,
-    grad_signal,
-    grad_gating,
-    grad_skip,
-    grad_w1,
-    grad_b1,
-    grad_w2,
-    grad_b2,
-    grad_w3,
+    load_sems,
     w1s,
     w2s,
     emb,
@@ -134,6 +168,51 @@
 ):
     me = lax.axis_index("seq")
     core = lax.axis_index("chan")
+    far = (
+        signal_far,
+        gating_far,
+        cotangent_far,
+        decay_far,
+        skip_row_far,
+        w1_far,
+        b1_far,
+        w2_far,
+        b2_far,
+        w3_far,
+        outer_hi_far,
+        outer_lo_far,
+        back_hi_far,
+        back_lo_far,
+        both_hi_far,
+        both_lo_far,
+        twist_cos_far,
+        twist_sin_far,
+    )
+    near = (
+        signal,
+        gating,
+        cotangent,
+        decay,
+        skip_row,
+        w1,
+        b1,
+        w2,
+        b2,
+        w3,
+        outer_hi,
+        outer_lo,
+        back_hi,
+        back_lo,
+        both_hi,
+        both_lo,
+        twist_cos,
+        twist_sin,
+    )
+    loads = [
+        pltpu.make_async_copy(far[at], near[at], load_sems.at[at]) for at in range(len(far))
+    ]
+    for load in loads:
+        load.start()
     barrier = pltpu.get_barrier_semaphore()
 
     @pl.loop(1, PARTS)
@@ -181,6 +260,9 @@
         return jnp.concatenate(
             [stage[:, 2 * q + h, plane * 128 : plane * 128 + 128] for h in range(2)], axis=1
         )
+
+    for load in loads:
+        load.wait()
 
     place(0, signal[...].astype(F32).T)
     dmixed_rows = cotangent[...].astype(F32) * gating[...].astype(F32)
@@ -259,6 +341,10 @@
     arrived(recv_a, 0)
     stage[...] = recv_a[...].astype(F32)
     skip_grads = []
+    channel = lax.broadcasted_iota(jnp.int32, (1, ROWS), 1)
+    skips = [
+        total(jnp.where(channel == me + q * PARTS, skip_row[...], 0.0)) for q in range(2)
+    ]
     for q in range(2):
         sig = take(0, q)
         high, low = take(1, q), take(2, q)
@@ -298,7 +384,7 @@
         put(0, q, high)
         put(1, q, conv - high)
         corr = inverse(filt_re * dm_re + filt_im * dm_im, filt_re * dm_im - filt_im * dm_re)
-        put(2, q, corr + skip_all[me + q * PARTS] * vals[q])
+        put(2, q, corr + skips[q] * vals[q])
     send_d[...] = stage[...].astype(BF)
     spread(lambda dst: send_d.at[dst], send_d.at[me], recv_d, 3)
 
@@ -355,9 +441,9 @@
     grad_w3[:, 0:128] = thirds[0:64]
     grad_w3[:, 128:256] = thirds[64:128]
     rest = recv_f[:, 1, :]
-    skips = rest.T
-    grad_skip[:, 0:128] = skips[64:65]
-    grad_skip[:, 128:256] = skips[65:66]
+    turned = rest.T
+    grad_skip[:, 0:128] = turned[64:65]
+    grad_skip[:, 128:256] = turned[65:66]
     grad_w1[1:33, :] = rest[0:32, 0:64]
     grad_w1[0:1, :] = rest[32:33, 0:64]
     grad_b1[...] = rest[33:34, 0:64]
@@ -385,8 +471,20 @@
     third_weight,
 ):
     vmem = pl.BlockSpec(memory_space=pltpu.VMEM)
-    smem = pl.BlockSpec(memory_space=pltpu.SMEM)
-    consts = [jnp.asarray(t) for t in tables()]
+    hbm = pl.BlockSpec(memory_space=pltpu.HBM)
+    operands = (
+        signal,
+        gating,
+        cotangent,
+        decay_rates.reshape(1, ROWS),
+        skip_gain.reshape(1, ROWS),
+        first_weight,
+        first_bias.reshape(1, FH),
+        second_weight,
+        second_bias.reshape(1, FH),
+        third_weight,
+        *[jnp.asarray(t) for t in tables()],
+    )
     wide_msg = pltpu.VMEM((PARTS, 4, 384), BF)
     thin_msg = pltpu.VMEM((PARTS, 4, 256), BF)
     pair = pltpu.VMEM((2, 128), F32)
@@ -403,9 +501,11 @@
             jax.ShapeDtypeStruct((1, FH), F32),
             jax.ShapeDtypeStruct((FH, ROWS), F32),
         ],
-        in_specs=[vmem] * 5 + [smem] + [vmem] * 13,
+        in_specs=[hbm] * 18,
         out_specs=[vmem] * 9,
-        scratch_shapes=[
+        scratch_shapes=[pltpu.VMEM(o.shape, o.dtype) for o in operands]
+        + [
+            pltpu.SemaphoreType.DMA((len(operands),)),
             pltpu.VMEM((40, FH), F32),
             pltpu.VMEM((72, FH), F32),
             pltpu.VMEM((40, ROWS), F32),
@@ -437,23 +537,20 @@
             pltpu.SemaphoreType.DMA((7,)),
         ],
         compiler_params=pltpu.CompilerParams(
-            collective_id=0, has_side_effects=True, vmem_limit_bytes=48 << 20
+            collective_id=0, has_side_effects=True, vmem_limit_bytes=LIMIT
         ),
         name="hyena",
-    )(
-        signal,
-        gating,
-        cotangent,
-        decay_rates.reshape(1, ROWS),
-        skip_gain.reshape(1, ROWS),
-        skip_gain,
-        first_weight,
-        first_bias.reshape(1, FH),
-        second_weight,
-        second_bias.reshape(1, FH),
-        third_weight,
-        *consts,
-    )
+    )(*operands)
+    results = pl.pallas_call(
+        deliver,
+        out_shape=[jax.ShapeDtypeStruct(r.shape, r.dtype) for r in results],
+        in_specs=[hbm] * 9,
+        out_specs=[hbm] * 9,
+        scratch_shapes=[pltpu.VMEM(r.shape, r.dtype) for r in results]
+        + [pltpu.SemaphoreType.DMA((9,)), pltpu.SemaphoreType.DMA((9,))],
+        compiler_params=pltpu.CompilerParams(vmem_limit_bytes=LIMIT),
+        name="deliver",
+    )(*results)
     out, g_sig, g_gate, g_skip, g_w1, g_b1, g_w2, g_b2, g_w3 = results
     return (
         out,

time: 85.7 us -> 68.8 us (0.80)
  local copies, waits for them, and re-layouts: 18.2 us -> 0 us
  Pallas kernels: 66.2 us -> 68 us
    unnamed x45 -> x0, local copies, waits for them, and re-layouts: 18.2 us -> none
    pallas_call x0 -> x1, Pallas kernels: none -> 1.9 us  [body(): pl.pallas_call(deliver, out_shape=[jax.ShapeDtypeStruct(r.shape, r.dtype)...]
where the time goes in v1:
time: 68.8 us; the launch traced here: 68.7 us
  Pallas kernels  68 us (99%)
    pallas_call x1, Pallas kernels, body(): pl.pallas_call(kernel, out_shape=[jax.ShapeDtypeStruct((ROWS, ROWS), BF),...  66.1 us
    pallas_call x1, Pallas kernels, body(): pl.pallas_call(deliver, out_shape=[jax.ShapeDtypeStruct(r.shape, r.dtype)...  1.9 us

profile of v1, /device:TPU:1, one launch (start us, length us, event | category | flops | bytes accessed | tf_op | source)
XLA Modules:
  0.0 68.7 jit_solution(1981615524715664225)
XLA Ops:
  0.6 66.1 %hyena.1 = (bf16[256,256]{1,0:T(8,128)(2,1)}, bf16[256,256]{1,0:T(8,128)(2,1)}, bf16[256,256]{1,0:T(8,128)(2,1)}, f32[1,256]{1,0:T(1,128)}, f32[33,64]{1,0:T(8,1...) custom-call(bf16[256,256]{1,0:T(8,128)(2,1)} %signal_far.1, ...), custom_call_target="tpu_custom_call" | custom-call | tf_op jit(solution)/shard_map/hyena/pallas_call | solution.py:491
  66.8 1.9 %deliver.1 = (bf16[256,256]{1,0:T(8,128)(2,1)}, bf16[256,256]{1,0:T(8,128)(2,1)}, bf16[256,256]{1,0:T(8,128)(2,1)}, f32[1,256]{1,0:T(1,128)}, f32[33,64]{1,0:T(8...) custom-call(bf16[256,256]{1,0:T(8,128)(2,1)} %get-tuple-element.27.refs_0_, ...), custom_call_target="tpu_custom_call" | custom-call | tf_op jit(solution)/shard_map/deliver/pallas_call | solution.py:544

commit v2 on v1

--- a/solution.py
+++ b/solution.py
@@ -108,15 +108,19 @@
     both_lo_far,
     twist_cos_far,
     twist_sin_far,
-    output,
-    grad_signal,
-    grad_gating,
+    output_far,
+    grad_signal_far,
+    grad_gating_far,
     grad_skip,
     grad_w1,
     grad_b1,
     grad_w2,
     grad_b2,
     grad_w3,
+    output,
+    grad_signal,
+    grad_gating,
+    store_sems,
     signal,
     gating,
     cotangent,
@@ -156,10 +160,16 @@
     recv_d,
     send_e,
     recv_e,
-    mine,
-    other,
+    mid,
+    mid_other,
+    send_g,
+    recv_g,
     send_f,
     recv_f,
+    send_s,
+    recv_s1,
+    recv_s,
+    shaped_keep,
     spec,
     vals,
     dfilt,
@@ -215,34 +225,69 @@
         load.start()
     barrier = pltpu.get_barrier_semaphore()
 
+    depth = me >> 4
+    plane_at = me & 15
+    mine = (plane_at << 3) + depth
+
     @pl.loop(1, PARTS)
     def _(step):
         pl.semaphore_signal(
-            barrier, inc=1, device_id={"seq": lax.rem(me + step, PARTS)}, device_id_type=MESH
+            barrier, inc=1, device_id={"seq": (me + step) & (PARTS - 1)}, device_id_type=MESH
         )
 
     pl.semaphore_signal(barrier, inc=1, device_id={"chan": 1 - core}, device_id_type=MESH)
 
-    def spread(src_of, own, recv, at):
+    def push(src, dst, at, device):
+        pltpu.make_async_remote_copy(
+            src_ref=src,
+            dst_ref=dst,
+            send_sem=send_sems.at[at],
+            recv_sem=recv_sems.at[at],
+            device_id=device,
+            device_id_type=MESH,
+        ).start()
+
+    def keep(src, dst, at):
+        pltpu.make_async_copy(src, dst, recv_sems.at[at]).start()
+
+    def inward(send, recv, at):
         @pl.loop(1, PARTS)
         def _(step):
-            dst = lax.rem(me + step, PARTS)
-            pltpu.make_async_remote_copy(
-                src_ref=src_of(dst),
-                dst_ref=recv.at[me],
-                send_sem=send_sems.at[at],
-                recv_sem=recv_sems.at[at],
-                device_id={"seq": dst},
-                device_id_type=MESH,
-            ).start()
-
-        pltpu.make_async_copy(own, recv.at[me], recv_sems.at[at]).start()
+            dst = (me + step) & (PARTS - 1)
+            push(send.at[((dst & 15) << 3) + (dst >> 4)], recv.at[me], at, {"seq": dst})
+
+        keep(send.at[mine], recv.at[me], at)
+
+    def outward(send, recv, at, first=0, last=PARTS):
+        @pl.loop(max(first, 1), last)
+        def _(step):
+            dst = (me + step) & (PARTS - 1)
+            push(send.at[dst], recv.at[mine], at, {"seq": dst})
+
+        if first == 0:
+            keep(send.at[me], recv.at[mine], at)
+
+    def over_depth(src_of, dst, at):
+        @pl.loop(1, 8)
+        def _(step):
+            peer = (depth + step) & 7
+            push(src_of(peer), dst, at, {"seq": (peer << 4) + plane_at})
+
+        keep(src_of(depth), dst, at)
+
+    def over_plane(src_of, dst, at):
+        @pl.loop(1, 16)
+        def _(step):
+            peer = (plane_at + step) & 15
+            push(src_of(peer), dst, at, {"seq": (depth << 4) + peer})
+
+        keep(src_of(plane_at), dst, at)
 
     def arrived(recv, at):
         pltpu.make_async_copy(recv, recv, recv_sems.at[at]).wait()
 
-    def left(recv, at):
-        rest = recv.at[pl.ds(0, PARTS - 1)]
+    def left(like, at, count=PARTS - 1):
+        rest = like.at[pl.ds(0, count)]
         pltpu.make_async_copy(rest, rest, send_sems.at[at]).wait()
 
     def place(plane, arr):
@@ -261,7 +306,7 @@
             [stage[:, 2 * q + h, plane * 128 : plane * 128 + 128] for h in range(2)], axis=1
         )
 
-    for load in loads:
+    for load in loads[:3]:
         load.wait()
 
     place(0, signal[...].astype(F32).T)
@@ -271,7 +316,11 @@
     place(1, high)
     place(2, wide[...] - high)
     send_a[...] = stage[...].astype(BF)
-
+    pl.semaphore_wait(barrier, PARTS)
+    inward(send_a, recv_a, 0)
+
+    for load in loads[3:]:
+        load.wait()
     stamp = me * ROWS + lax.broadcasted_iota(jnp.int32, (BANDS, ROWS), 1)
     band = lax.broadcasted_iota(jnp.int32, (BANDS, ROWS), 0) + 1
     phase = ((stamp * band) & (LENGTH - 1)).astype(F32) * (full_turn / LENGTH)
@@ -296,15 +345,12 @@
     cos2[...] = jnp.cos(pre2)
     rates = jnp.broadcast_to(decay[...], (ROWS, ROWS)).T
     fade[...] = jnp.exp(-jnp.broadcast_to(ramp[0:1], (ROWS, ROWS)) * rates)
-    wide[...] = contract(w3[...], second[...], (0, 0), lax.Precision.HIGHEST) * fade[...]
-    high = wide[...].astype(BF).astype(F32)
+    shaped_keep[...] = contract(w3[...], second[...], (0, 0), lax.Precision.HIGHEST) * fade[...]
+    high = shaped_keep[...].astype(BF).astype(F32)
     place(0, high)
-    place(1, wide[...] - high)
+    place(1, shaped_keep[...] - high)
     send_b[...] = stage[:, :, 0:256].astype(BF)
-
-    pl.semaphore_wait(barrier, PARTS)
-    spread(lambda dst: send_a.at[dst], send_a.at[me], recv_a, 0)
-    spread(lambda dst: send_b.at[dst], send_b.at[me], recv_b, 1)
+    inward(send_b, recv_b, 1)
 
     both = (both_hi, both_lo)
 
@@ -343,7 +389,7 @@
     skip_grads = []
     channel = lax.broadcasted_iota(jnp.int32, (1, ROWS), 1)
     skips = [
-        total(jnp.where(channel == me + q * PARTS, skip_row[...], 0.0)) for q in range(2)
+        total(jnp.where(channel == mine + q * PARTS, skip_row[...], 0.0)) for q in range(2)
     ]
     for q in range(2):
         sig = take(0, q)
@@ -356,23 +402,29 @@
         sig_re, sig_im, dm_re, dm_im = spec[q, 0], spec[q, 1], spec[2 + q, 0], spec[2 + q, 1]
         dfilt[q] = inverse(sig_re * dm_re + sig_im * dm_im, sig_re * dm_im - sig_im * dm_re)
 
-    arrived(recv_b, 1)
-    stage[:, :, 0:256] = recv_b[...].astype(F32)
-    filters, scales = [], []
-    for q in range(2):
-        high, low = take(0, q), take(1, q)
-        shaped = high + low
-        scale = 1.0 / jnp.sqrt(total(shaped * shaped) + norm_eps)
-        filt = shaped * scale
-        filters.append((high.astype(BF), low.astype(BF)))
-        scales.append(scale)
-        dfilt[q] = (dfilt[q] - filt * total(filt * dfilt[q])) * scale
     for q in range(2):
         high = dfilt[q].astype(BF).astype(F32)
         put(0, q, high)
         put(1, q, dfilt[q] - high)
     send_c[...] = stage[:, :, 0:256].astype(BF)
-    spread(lambda dst: send_c.at[dst], send_c.at[me], recv_c, 2)
+    outward(send_c, recv_c, 2, 0, 72)
+
+    arrived(recv_b, 1)
+    stage[:, :, 0:256] = recv_b[...].astype(F32)
+    lane = lax.broadcasted_iota(jnp.int32, (1, 128), 1)
+    filters, scales = [], []
+    scalars = jnp.zeros((1, 128), F32)
+    for q in range(2):
+        high, low = take(0, q), take(1, q)
+        shaped = high + low
+        scale = 1.0 / jnp.sqrt(total(shaped * shaped) + norm_eps)
+        pull = total(shaped * scale * dfilt[q]) * scale * scale
+        filters.append((high.astype(BF), low.astype(BF)))
+        scales.append(scale)
+        scalars = jnp.where(lane == 2 * q, scale, jnp.where(lane == 2 * q + 1, pull, scalars))
+    send_s[...] = scalars
+    over_depth(lambda peer: send_s, recv_s1.at[depth], 7)
+    outward(send_c, recv_c, 2, 72, PARTS)
 
     for q in range(2):
         forward(4 + q, filters[q])
@@ -386,13 +438,19 @@
         corr = inverse(filt_re * dm_re + filt_im * dm_im, filt_re * dm_im - filt_im * dm_re)
         put(2, q, corr + skips[q] * vals[q])
     send_d[...] = stage[...].astype(BF)
-    spread(lambda dst: send_d.at[dst], send_d.at[me], recv_d, 3)
+    arrived(recv_s1, 7)
+    over_plane(lambda peer: recv_s1, recv_s.at[pl.ds(plane_at * 8, 8)], 8)
+    outward(send_d, recv_d, 3, 0, 72)
 
     arrived(recv_c, 2)
+    arrived(recv_s, 8)
     stage[:, :, 0:256] = recv_c[...].astype(F32)
-    for q in range(2):
-        wide[q * 128 : q * 128 + 128, :] = take(0, q) + take(1, q)
-    wide[...] = wide[...] * fade[...]
+    factors = recv_s[:, 0, :]
+    for q in range(2):
+        at = pl.ds(q * 128, 128)
+        scale, pull = factors[:, 2 * q : 2 * q + 1], factors[:, 2 * q + 1 : 2 * q + 2]
+        dshaped = (take(0, q) + take(1, q)) * scale - shaped_keep[at, :] * pull
+        wide[at, :] = dshaped * fade[at, :]
     draw = wide[...]
     third = contract(draw, second[...], (1, 1), lax.Precision.HIGH)
     dpre2 = contract(w3[...], draw, (1, 0), lax.Precision.HIGH) * cos2[...]
@@ -402,28 +460,28 @@
     send_e[:, 0, :] = jnp.concatenate([third[0:128], third[128:256]], axis=1)
     shared = jnp.concatenate([grad1, grad2, jnp.zeros((16, FH), F32)], axis=0)
     send_e[:, 1, :] = jnp.concatenate([shared, jnp.zeros((128, FH), F32)], axis=1)
-    spread(lambda dst: send_e.at[dst], send_e.at[me], recv_e, 4)
+    over_plane(lambda peer: send_e.at[pl.ds(peer * 8, 8)], recv_e.at[plane_at], 4)
+    outward(send_d, recv_d, 3, 72, PARTS)
     arrived(recv_e, 4)
-    summed = jnp.sum(recv_e[...], axis=0)
-    mine[...] = summed
-    swap = pltpu.make_async_remote_copy(
-        src_ref=mine,
-        dst_ref=other,
-        send_sem=send_sems.at[5],
-        recv_sem=recv_sems.at[5],
-        device_id={"chan": 1 - core},
-        device_id_type=MESH,
-    )
-    swap.start()
-    swap.wait()
-    lane = lax.broadcasted_iota(jnp.int32, (1, 128), 1)
-    send_f[0:1, :] = summed[0:1]
-    send_f[1:2, :] = jnp.where(
-        lane < FH,
-        summed[1:2] + other[1:2, :],
-        jnp.where(lane == FH, skip_grads[0], skip_grads[1]),
-    )
-    spread(lambda dst: send_f, send_f, recv_f, 6)
+    part = jnp.sum(recv_e[...], axis=0)
+    mid[...] = part
+    push(mid, mid_other, 5, {"chan": 1 - core})
+    owner = lax.broadcasted_iota(jnp.int32, (8, 2, 128), 0)
+    row = lax.broadcasted_iota(jnp.int32, (8, 2, 128), 1)
+    column = lax.broadcasted_iota(jnp.int32, (8, 2, 128), 2)
+    here = (owner == depth) & (row == 1)
+    extra = jnp.where(
+        here & (column == FH),
+        skip_grads[0][None],
+        jnp.where(here & (column == FH + 1), skip_grads[1][None], 0.0),
+    )
+    arrived(mid_other, 5)
+    both_cores = (row == 1) & (column < FH)
+    send_g[...] = part + jnp.where(both_cores, mid_other[...], extra)
+    over_depth(lambda peer: send_g, recv_g.at[depth], 6)
+    arrived(recv_g, 6)
+    send_f[...] = jnp.sum(recv_g[...], axis=0)
+    over_plane(lambda peer: send_f, recv_f.at[pl.ds(plane_at * 8, 8)], 10)
 
     arrived(recv_d, 3)
     stage[...] = recv_d[...].astype(F32)
@@ -436,7 +494,14 @@
         wide[q * 128 : q * 128 + 128, :] = take(2, q)
     grad_signal[...] = wide[...].T.astype(BF)
 
-    arrived(recv_f, 6)
+    stores = [
+        pltpu.make_async_copy(output, output_far, store_sems.at[0]),
+        pltpu.make_async_copy(grad_signal, grad_signal_far, store_sems.at[1]),
+        pltpu.make_async_copy(grad_gating, grad_gating_far, store_sems.at[2]),
+    ]
+    for store in stores:
+        store.start()
+    arrived(recv_f, 10)
     thirds = recv_f[:, 0, :].T
     grad_w3[:, 0:128] = thirds[0:64]
     grad_w3[:, 128:256] = thirds[64:128]
@@ -450,12 +515,18 @@
     grad_w2[...] = rest[40:104, 0:64]
     grad_b2[...] = rest[104:105, 0:64]
 
+    for store in stores:
+        store.wait()
     left(send_a, 0)
     left(send_b, 1)
     left(send_c, 2)
     left(send_d, 3)
-    left(send_e, 4)
-    left(recv_f, 6)
+    left(send_e, 4, 120)
+    left(mid, 5, 8)
+    left(recv_g, 6, 7)
+    left(recv_s1, 7, 7)
+    left(recv_s, 8, 120)
+    left(recv_f, 10, 120)
 
 
 def body(
@@ -487,7 +558,6 @@
     )
     wide_msg = pltpu.VMEM((PARTS, 4, 384), BF)
     thin_msg = pltpu.VMEM((PARTS, 4, 256), BF)
-    pair = pltpu.VMEM((2, 128), F32)
     results = pl.pallas_call(
         kernel,
         out_shape=[
@@ -502,8 +572,10 @@
             jax.ShapeDtypeStruct((FH, ROWS), F32),
         ],
         in_specs=[hbm] * 18,
-        out_specs=[vmem] * 9,
-        scratch_shapes=[pltpu.VMEM(o.shape, o.dtype) for o in operands]
+        out_specs=[hbm] * 3 + [vmem] * 6,
+        scratch_shapes=[pltpu.VMEM((ROWS, ROWS), BF)] * 3
+        + [pltpu.SemaphoreType.DMA((3,))]
+        + [pltpu.VMEM(o.shape, o.dtype) for o in operands]
         + [
             pltpu.SemaphoreType.DMA((len(operands),)),
             pltpu.VMEM((40, FH), F32),
@@ -525,16 +597,22 @@
             wide_msg,
             wide_msg,
             pltpu.VMEM((PARTS, 2, 128), F32),
+            pltpu.VMEM((16, 8, 2, 128), F32),
+            pltpu.VMEM((8, 2, 128), F32),
+            pltpu.VMEM((8, 2, 128), F32),
+            pltpu.VMEM((8, 2, 128), F32),
+            pltpu.VMEM((8, 8, 2, 128), F32),
+            pltpu.VMEM((8, 2, 128), F32),
             pltpu.VMEM((PARTS, 2, 128), F32),
-            pair,
-            pair,
-            pair,
-            pltpu.VMEM((PARTS, 2, 128), F32),
+            pltpu.VMEM((1, 128), F32),
+            pltpu.VMEM((8, 1, 128), F32),
+            pltpu.VMEM((PARTS, 1, 128), F32),
+            pltpu.VMEM((ROWS, ROWS), F32),
             pltpu.VMEM((6, 2, HALF, ROWS), F32),
             pltpu.VMEM((2, PARTS, ROWS), F32),
             pltpu.VMEM((2, PARTS, ROWS), F32),
-            pltpu.SemaphoreType.DMA((7,)),
-            pltpu.SemaphoreType.DMA((7,)),
+            pltpu.SemaphoreType.DMA((11,)),
+            pltpu.SemaphoreType.DMA((11,)),
         ],
         compiler_params=pltpu.CompilerParams(
             collective_id=0, has_side_effects=True, vmem_limit_bytes=LIMIT

time: 68.8 us -> 64.8 us (0.942)
  Pallas kernels: 68 us -> 64.1 us
    pallas_call x1, Pallas kernels: 66.1 us -> 62.2 us  [body(): pl.pallas_call(kernel, out_shape=[jax.ShapeDtypeStruct((ROWS, ROWS), BF),...]
where the time goes in v2:
time: 64.8 us; the launch traced here: 64.7 us
  Pallas kernels  64.1 us (99%)
  between operations  0.65 us (1%)
    pallas_call x1, Pallas kernels, body(): pl.pallas_call(kernel, out_shape=[jax.ShapeDtypeStruct((ROWS, ROWS), BF),...  62.2 us
    pallas_call x1, Pallas kernels, body(): pl.pallas_call(deliver, out_shape=[jax.ShapeDtypeStruct(r.shape, r.dtype)...  1.9 us

profile of v2, /device:TPU:1, one launch (start us, length us, event | category | flops | bytes accessed | tf_op | source)
XLA Modules:
  0.0 64.7 jit_solution(1016202013695064924)
XLA Ops:
  0.6 62.2 %hyena.1 = (bf16[256,256]{1,0:T(8,128)(2,1)}, bf16[256,256]{1,0:T(8,128)(2,1)}, bf16[256,256]{1,0:T(8,128)(2,1)}, f32[1,256]{1,0:T(1,128)}, f32[33,64]{1,0:T(8,1...) custom-call(bf16[256,256]{1,0:T(8,128)(2,1)} %signal_far.1, ...), custom_call_target="tpu_custom_call" | custom-call | tf_op jit(solution)/shard_map/hyena/pallas_call | solution.py:561
  62.8 1.9 %deliver.1 = (bf16[256,256]{1,0:T(8,128)(2,1)}, bf16[256,256]{1,0:T(8,128)(2,1)}, bf16[256,256]{1,0:T(8,128)(2,1)}, f32[1,256]{1,0:T(1,128)}, f32[33,64]{1,0:T(8...) custom-call(bf16[256,256]{1,0:T(8,128)(2,1)} %get-tuple-element.27.refs_0_, ...), custom_call_target="tpu_custom_call" | custom-call | tf_op jit(solution)/shard_map/deliver/pallas_call | solution.py:622

commit v3 on v2

--- a/solution.py
+++ b/solution.py
@@ -221,21 +221,29 @@
     loads = [
         pltpu.make_async_copy(far[at], near[at], load_sems.at[at]) for at in range(len(far))
     ]
-    for load in loads:
-        load.start()
-    barrier = pltpu.get_barrier_semaphore()
 
     depth = me >> 4
     plane_at = me & 15
     mine = (plane_at << 3) + depth
-
-    @pl.loop(1, PARTS)
-    def _(step):
-        pl.semaphore_signal(
-            barrier, inc=1, device_id={"seq": (me + step) & (PARTS - 1)}, device_id_type=MESH
-        )
-
+    barrier = pltpu.get_barrier_semaphore()
+
+    far_half, near_half = (4, 3, 5, 2), (6, 1, 7, 0)
+
+    def each(steps, visit):
+        for ahead in steps:
+            base = ((depth + ahead) & 7) << 4
+
+            @pl.loop(1 if ahead == 0 else 0, 16)
+            def _(step):
+                visit(base + ((plane_at + (step if ahead == 0 else 10 + step)) & 15))
+
+    def greet(dst):
+        pl.semaphore_signal(barrier, inc=1, device_id={"seq": dst}, device_id_type=MESH)
+
+    each(far_half + near_half, greet)
     pl.semaphore_signal(barrier, inc=1, device_id={"chan": 1 - core}, device_id_type=MESH)
+    for load in loads:
+        load.start()
 
     def push(src, dst, at, device):
         pltpu.make_async_remote_copy(
@@ -251,20 +259,15 @@
         pltpu.make_async_copy(src, dst, recv_sems.at[at]).start()
 
     def inward(send, recv, at):
-        @pl.loop(1, PARTS)
-        def _(step):
-            dst = (me + step) & (PARTS - 1)
+        def visit(dst):
             push(send.at[((dst & 15) << 3) + (dst >> 4)], recv.at[me], at, {"seq": dst})
 
+        each(far_half + near_half, visit)
         keep(send.at[mine], recv.at[me], at)
 
-    def outward(send, recv, at, first=0, last=PARTS):
-        @pl.loop(max(first, 1), last)
-        def _(step):
-            dst = (me + step) & (PARTS - 1)
-            push(send.at[dst], recv.at[mine], at, {"seq": dst})
-
-        if first == 0:
+    def outward(send, recv, at, steps):
+        each(steps, lambda dst: push(send.at[dst], recv.at[mine], at, {"seq": dst}))
+        if 0 in steps:
             keep(send.at[me], recv.at[mine], at)
 
     def over_depth(src_of, dst, at):
@@ -407,7 +410,7 @@
         put(0, q, high)
         put(1, q, dfilt[q] - high)
     send_c[...] = stage[:, :, 0:256].astype(BF)
-    outward(send_c, recv_c, 2, 0, 72)
+    outward(send_c, recv_c, 2, far_half)
 
     arrived(recv_b, 1)
     stage[:, :, 0:256] = recv_b[...].astype(F32)
@@ -417,14 +420,15 @@
     for q in range(2):
         high, low = take(0, q), take(1, q)
         shaped = high + low
+        along = total(shaped * dfilt[q])
         scale = 1.0 / jnp.sqrt(total(shaped * shaped) + norm_eps)
-        pull = total(shaped * scale * dfilt[q]) * scale * scale
+        pull = along * scale * scale * scale
         filters.append((high.astype(BF), low.astype(BF)))
         scales.append(scale)
         scalars = jnp.where(lane == 2 * q, scale, jnp.where(lane == 2 * q + 1, pull, scalars))
     send_s[...] = scalars
     over_depth(lambda peer: send_s, recv_s1.at[depth], 7)
-    outward(send_c, recv_c, 2, 72, PARTS)
+    outward(send_c, recv_c, 2, near_half)
 
     for q in range(2):
         forward(4 + q, filters[q])
@@ -440,17 +444,20 @@
     send_d[...] = stage[...].astype(BF)
     arrived(recv_s1, 7)
     over_plane(lambda peer: recv_s1, recv_s.at[pl.ds(plane_at * 8, 8)], 8)
-    outward(send_d, recv_d, 3, 0, 72)
+    outward(send_d, recv_d, 3, far_half)
 
     arrived(recv_c, 2)
+    stage[:, :, 0:256] = recv_c[...].astype(F32)
+    for q in range(2):
+        at = pl.ds(q * 128, 128)
+        wide[at, :] = (take(0, q) + take(1, q)) * fade[at, :]
+    shaped_keep[...] = shaped_keep[...] * fade[...]
     arrived(recv_s, 8)
-    stage[:, :, 0:256] = recv_c[...].astype(F32)
     factors = recv_s[:, 0, :]
     for q in range(2):
         at = pl.ds(q * 128, 128)
         scale, pull = factors[:, 2 * q : 2 * q + 1], factors[:, 2 * q + 1 : 2 * q + 2]
-        dshaped = (take(0, q) + take(1, q)) * scale - shaped_keep[at, :] * pull
-        wide[at, :] = dshaped * fade[at, :]
+        wide[at, :] = wide[at, :] * scale - shaped_keep[at, :] * pull
     draw = wide[...]
     third = contract(draw, second[...], (1, 1), lax.Precision.HIGH)
     dpre2 = contract(w3[...], draw, (1, 0), lax.Precision.HIGH) * cos2[...]
@@ -461,7 +468,7 @@
     shared = jnp.concatenate([grad1, grad2, jnp.zeros((16, FH), F32)], axis=0)
     send_e[:, 1, :] = jnp.concatenate([shared, jnp.zeros((128, FH), F32)], axis=1)
     over_plane(lambda peer: send_e.at[pl.ds(peer * 8, 8)], recv_e.at[plane_at], 4)
-    outward(send_d, recv_d, 3, 72, PARTS)
+    outward(send_d, recv_d, 3, near_half)
     arrived(recv_e, 4)
     part = jnp.sum(recv_e[...], axis=0)
     mid[...] = part

time: 64.8 us -> 63.1 us (0.974)
  Pallas kernels: 64.1 us -> 62.3 us
    pallas_call x1, Pallas kernels: 62.2 us -> 60.5 us  [body(): pl.pallas_call(kernel, out_shape=[jax.ShapeDtypeStruct((ROWS, ROWS), BF),...]
where the time goes in v3:
time: 63.1 us; the launch traced here: 63 us
  Pallas kernels  62.3 us (99%)
  between operations  0.65 us (1%)
    pallas_call x1, Pallas kernels, body(): pl.pallas_call(kernel, out_shape=[jax.ShapeDtypeStruct((ROWS, ROWS), BF),...  60.5 us
    pallas_call x1, Pallas kernels, body(): pl.pallas_call(deliver, out_shape=[jax.ShapeDtypeStruct(r.shape, r.dtype)...  1.9 us

profile of v3, /device:TPU:1, one launch (start us, length us, event | category | flops | bytes accessed | tf_op | source)
XLA Modules:
  0.0 63.0 jit_solution(15832587822035098544)
XLA Ops:
  0.6 60.5 %hyena.1 = (bf16[256,256]{1,0:T(8,128)(2,1)}, bf16[256,256]{1,0:T(8,128)(2,1)}, bf16[256,256]{1,0:T(8,128)(2,1)}, f32[1,256]{1,0:T(1,128)}, f32[33,64]{1,0:T(8,1...) custom-call(bf16[256,256]{1,0:T(8,128)(2,1)} %signal_far.1, ...), custom_call_target="tpu_custom_call" | custom-call | tf_op jit(solution)/shard_map/hyena/pallas_call | solution.py:568
  61.1 1.9 %deliver.1 = (bf16[256,256]{1,0:T(8,128)(2,1)}, bf16[256,256]{1,0:T(8,128)(2,1)}, bf16[256,256]{1,0:T(8,128)(2,1)}, f32[1,256]{1,0:T(1,128)}, f32[33,64]{1,0:T(8...) custom-call(bf16[256,256]{1,0:T(8,128)(2,1)} %get-tuple-element.27.refs_0_, ...), custom_call_target="tpu_custom_call" | custom-call | tf_op jit(solution)/shard_map/deliver/pallas_call | solution.py:629

commit v4 on v3

--- a/solution.py
+++ b/solution.py
@@ -271,18 +271,19 @@
             keep(send.at[me], recv.at[mine], at)
 
     def over_depth(src_of, dst, at):
-        @pl.loop(1, 8)
-        def _(step):
-            peer = (depth + step) & 7
+        for ahead in (4, 3, 5, 2, 6, 1, 7):
+            peer = (depth + ahead) & 7
             push(src_of(peer), dst, at, {"seq": (peer << 4) + plane_at})
-
         keep(src_of(depth), dst, at)
 
     def over_plane(src_of, dst, at):
-        @pl.loop(1, 16)
-        def _(step):
-            peer = (plane_at + step) & 15
-            push(src_of(peer), dst, at, {"seq": (depth << 4) + peer})
+        for ahead in (2, 1, 3, 0):
+            base = (((plane_at >> 2) + ahead) & 3) << 2
+
+            @pl.loop(1 if ahead == 0 else 0, 4)
+            def _(step):
+                peer = base + ((plane_at + (step if ahead == 0 else 2 + step)) & 3)
+                push(src_of(peer), dst, at, {"seq": (depth << 4) + peer})
 
         keep(src_of(plane_at), dst, at)
 

time: 63.1 us -> 62.6 us (level)
  no operation moved by 1% of the time
where the time goes in v4:
time: 62.6 us; the launch traced here: 62.5 us
  Pallas kernels  61.8 us (99%)
  between operations  0.65 us (1%)
    pallas_call x1, Pallas kernels, body(): pl.pallas_call(kernel, out_shape=[jax.ShapeDtypeStruct((ROWS, ROWS), BF),...  59.9 us
    pallas_call x1, Pallas kernels, body(): pl.pallas_call(deliver, out_shape=[jax.ShapeDtypeStruct(r.shape, r.dtype)...  1.9 us

profile of v4, /device:TPU:1, one launch (start us, length us, event | category | flops | bytes accessed | tf_op | source)
XLA Modules:
  0.0 62.5 jit_solution(13006945988166157002)
XLA Ops:
  0.6 59.9 %hyena.1 = (bf16[256,256]{1,0:T(8,128)(2,1)}, bf16[256,256]{1,0:T(8,128)(2,1)}, bf16[256,256]{1,0:T(8,128)(2,1)}, f32[1,256]{1,0:T(1,128)}, f32[33,64]{1,0:T(8,1...) custom-call(bf16[256,256]{1,0:T(8,128)(2,1)} %signal_far.1, ...), custom_call_target="tpu_custom_call" | custom-call | tf_op jit(solution)/shard_map/hyena/pallas_call | solution.py:569
  60.6 1.9 %deliver.1 = (bf16[256,256]{1,0:T(8,128)(2,1)}, bf16[256,256]{1,0:T(8,128)(2,1)}, bf16[256,256]{1,0:T(8,128)(2,1)}, f32[1,256]{1,0:T(1,128)}, f32[33,64]{1,0:T(8...) custom-call(bf16[256,256]{1,0:T(8,128)(2,1)} %get-tuple-element.27.refs_0_, ...), custom_call_target="tpu_custom_call" | custom-call | tf_op jit(solution)/shard_map/deliver/pallas_call | solution.py:630
